TPU v7x, 128 devices: a whole 4x4x4 slice. The times are simulated.
128 devices in a mesh: row: 2 (over y_lo), col: 8 (over x, core), layer: 8 (over y_hi, z).
Axes of the slice: x: 4, y: 4 (y_hi: 2, y_lo: 2; y = y_hi * 2 + y_lo), z: 4, core: 2. Of those that a mesh axis runs over, the one named last changes fastest.
Arguments:
- left: float32 [1024, 8192], P('row', ('layer', 'col')), may hold values from -6 to 6
- right: float32 [8192, 16384], P(('layer', 'row'), 'col'), may hold values from -0.125 to 0.125
- left_mask: int32 [2, 16], replicated, may hold values 0 or 1
- right_mask: int32 [16, 32], replicated, may hold values 0 or 1
- result_mask: int32 [2, 32], replicated, may hold values 0 or 1
Outputs:
- ladder: float32 [1024, 16384], P('row', ('col', 'layer'))
Inputs may be any that keep to these rules, and one draw needn't show every extreme that they name: `left_mask`: 1 marks a present tile, 0 an absent one. `right_mask`: 1 marks a present tile, 0 an absent one. `result_mask`: 1 marks a present tile, 0 an absent one.
All inputs are finite; a program needn't handle non-finite values.
Results may differ from a plain program's by a relative error of at most 0.0003.
Values sent between devices are 32-bit elements; how exact they have to be, the bound alone decides.
No kernel may reach another device: no remote copies, remote signals or barrier semaphores. Data moves between devices by JAX's collectives and lax.ppermute only.
A program may use at most 64 MiB of HBM per device.

v0:
```python
import jax
import jax.numpy as jnp
from jax import lax
from jax.experimental import pallas as pl
from jax.experimental.pallas import tpu as pltpu
from jax.sharding import Mesh
from jax.sharding import PartitionSpec as P

TILE = 512
WIDTH = 256
AXES = ("yl", "x", "c", "yh", "z")
SIZES = (2, 4, 2, 2, 4)
ROWS = {"A": 256, "B": 256}
COST = {"split": 1, "first": 1, "second": 1, "join_a": 1, "join_b": 1, "last": 1}
SMEM = pl.BlockSpec(memory_space=pltpu.SMEM)
VMEM = pl.BlockSpec(memory_space=pltpu.VMEM)


def permute(value, yl=0, x=0, c=0, yh=0, z=0):
    bits = (((yl * 4 + x) * 2 + c) * 2 + yh) * 4 + z
    return lax.ppermute(value, AXES, [(n, n ^ bits) for n in range(128)])


def along_y(value, bits):
    return permute(value, yl=bits % 2, yh=bits // 2)


def along_z(value, bits):
    return permute(value, z=bits)


def settings(cost):
    size = 48 if cost == "split" else 8
    return dict(
        compiler_params=pltpu.CompilerParams(vmem_limit_bytes=size * 2**20),
        cost_estimate=pl.CostEstimate(flops=1, bytes_accessed=COST[cost], transcendentals=0),
    )


def split_kernel(spots, left_mask, right_mask, result_mask, right, hi_ref, lo_ref, tiles, sems):
    yl, x, c, yh, z = (spots[n] for n in range(5))
    k = (yh * 4 + z) * 2 + yl
    first = (x * 2 + c) * 4

    def block(n):
        chunk = lax.rem(yh + n // 4, 2) * 4 + jnp.bitwise_xor(z, n % 4)
        j = first + lax.div(chunk, 2)
        used = right_mask[k, j] * (left_mask[0, k] * result_mask[0, j] + left_mask[1, k] * result_mask[1, j]) > 0
        where = pl.ds(pl.multiple_of(chunk * WIDTH, WIDTH), WIDTH)
        return used, pltpu.make_async_copy(right.at[:, where], tiles.at[n], sems.at[n])

    for n in range(8):
        used, copy = block(n)

        @pl.when(used)
        def _():
            copy.start()

    for n in range(8):
        used, copy = block(n)

        @pl.when(used)
        def _():
            copy.wait()
            tile = tiles[n]
            hi = tile.astype(jnp.bfloat16)
            hi_ref[n] = hi
            lo_ref[n] = (tile - hi.astype(jnp.float32)).astype(jnp.bfloat16)


def split(spots, masks, right):
    return pl.pallas_call(
        split_kernel,
        out_shape=[jax.ShapeDtypeStruct((8, TILE, WIDTH), jnp.bfloat16)] * 2,
        in_specs=[SMEM] * 4 + [pl.BlockSpec(memory_space=pltpu.HBM)],
        out_specs=[VMEM] * 2,
        scratch_shapes=[pltpu.VMEM((8, TILE, WIDTH), jnp.float32), pltpu.SemaphoreType.DMA((8,))],
        **settings("split"),
    )(spots, *masks, right)


def product_kernel(turns_all, plan, blocks, spots, left_mask, right_mask, result_mask, *rest):
    pieces, right, outs, (hi_ref, lo_ref) = rest[:blocks], rest[blocks : blocks + 2], rest[blocks + 2 : -2], rest[-2:]
    yl, x, c, yh, z = (spots[n] for n in range(5))
    k = (yh * 4 + z) * 2 + yl
    first = (x * 2 + c) * 4
    near = 1 - lax.rem(x, 2)

    def used(dy, chunk):
        i = lax.rem(yl + dy % 2, 2)
        j = first + lax.div(chunk, 2)
        return left_mask[i, k] * right_mask[k, j] * result_mask[i, j] > 0

    groups = [
        (n, lax.rem(yh + high, 2) * 4 + jnp.bitwise_xor(z, dz), [dy for dy in turns_all if dy // 2 == high], dz)
        for n, (high, dz) in enumerate((high, dz) for high in range(2) for dz in range(4))
    ]

    if blocks == 2:
        cores = [(c, pieces[0]), (1 - c, pieces[1])]
    else:
        cores = [(core, pieces[0].at[core]) for core in range(2)]
    for core, piece in cores:
        for n, chip in enumerate((near, 1 - near)):
            value = piece[n]
            hi = value.astype(jnp.bfloat16)
            where = pl.ds(pl.multiple_of(chip * 256 + core * 128, 128), 128)
            hi_ref[:, where] = hi
            lo_ref[:, where] = (value - hi.astype(jnp.float32)).astype(jnp.bfloat16)
    for n, chunk, turns, dz in groups:

        for dy in turns:

            @pl.when(used(dy, chunk))
            def _():
                hi, lo = right[0][n], right[1][n]
                total = jnp.dot(hi_ref[...], hi, preferred_element_type=jnp.float32)
                total += jnp.dot(hi_ref[...], lo, preferred_element_type=jnp.float32)
                total += jnp.dot(lo_ref[...], hi, preferred_element_type=jnp.float32)
                done = 0
                for half, out, slot in plan[dy, dz]:
                    outs[out][slot] = total[done : done + ROWS[half]]
                    done += ROWS[half]

            @pl.when(jnp.logical_not(used(dy, chunk)))
            def _():
                for half, out, slot in plan[dy, dz]:
                    outs[out][slot] = jnp.zeros((ROWS[half], WIDTH), jnp.float32)


def product(turns, names, spots, masks, pieces, right, cost):
    plan = {
        (dy, dz): [
            (half, n, blocks.index((half, dy, dz)))
            for half in "AB"
            for n, blocks in enumerate(names.values())
            if (half, dy, dz) in blocks
        ]
        for dy in turns
        for dz in range(4)
    }
    outs = pl.pallas_call(
        lambda *refs: product_kernel(turns, plan, len(pieces), *refs),
        out_shape=[jax.ShapeDtypeStruct((len(b), ROWS[b[0][0]], WIDTH), jnp.float32) for b in names.values()],
        in_specs=[SMEM] * 4 + [VMEM] * (len(pieces) + 2),
        out_specs=[VMEM] * len(names),
        scratch_shapes=[pltpu.VMEM((TILE, TILE), jnp.bfloat16)] * 2,
        **settings(cost),
    )(spots, *masks, *pieces, *right)
    return dict(zip(names, outs))


def join(value, first, arrived, cost, kept=None):
    def kernel(value_ref, arrived_ref, *rest):
        out_ref = rest[-1]
        del value_ref
        for n in range(count):
            out_ref[first + n] = (rest[0][n] if kept is not None else out_ref[first + n]) + arrived_ref[n]

    count = min(value.shape[0] - first, arrived.shape[0])
    operands = [value, arrived] + ([] if kept is None else [kept])
    return pl.pallas_call(
        kernel,
        out_shape=jax.ShapeDtypeStruct(value.shape, value.dtype),
        in_specs=[VMEM] * len(operands),
        out_specs=VMEM,
        input_output_aliases={0: 0},
        **settings(cost),
    )(*operands)


def total(top, bottom):
    def kernel(*refs):
        out_ref = refs[-1]
        out_ref[: ROWS["A"]] = sum(ref[...] for ref in refs[1 : len(top)]) + refs[0][...]
        out_ref[ROWS["A"] :] = sum(ref[...] for ref in refs[len(top) + 1 : -1]) + refs[len(top)][...]

    return pl.pallas_call(
        kernel,
        out_shape=jax.ShapeDtypeStruct((TILE, WIDTH), jnp.float32),
        in_specs=[VMEM] * (len(top) + len(bottom)),
        **settings("last"),
    )(*top, *bottom)


def both_cores(value):
    return lax.all_to_all(jnp.broadcast_to(value[None], (2, *value.shape)), "c", 0, 0, tiled=True)


def shards(left, right, left_mask, right_mask, result_mask):
    yl, x, c, yh, z = (lax.axis_index(a) for a in AXES)
    spots = jnp.stack([yl, x, c, yh, z]).astype(jnp.int32)
    masks = (left_mask, right_mask, result_mask)

    here = x // 2 == yl
    across, beside, between = (permute(left, x=bits) for bits in (2, 3, 1))
    right = split(spots, masks, right)
    across, right = lax.optimization_barrier((across, right))
    mine = jnp.stack([jnp.where(here, between, beside), jnp.where(here, left, across)])
    others = jnp.stack([jnp.where(here, beside, between), jnp.where(here, across, left)])
    others = along_y(others, 1)
    p = product(
        (0, 2),
        {
            "y1": [("A", 2, 0)],
            "y3": [("A", 2, 1), ("A", 2, 2), ("A", 2, 3)],
            "z1": [("B", 0, 2), ("B", 0, 1)],
            "z3": [("B", 2, 2), ("B", 2, 3)],
            "z1_kept": [("B", 2, 1)],
            "z3_kept": [("B", 0, 3)],
            "a": [("A", 0, d) for d in range(4)],
            "b": [("B", 0, 0), ("B", 2, 0)],
        },
        spots,
        masks,
        (mine, permute(mine, c=1)),
        right,
        "first",
    )
    from_y1 = along_y(p["y1"], 1)
    from_y3 = along_y(p["y3"], 3)
    from_z1 = along_z(p["z1"], 1)
    from_z3 = along_z(p["z3"], 3)
    others, a_own = lax.optimization_barrier((others, p["a"]))
    others, from_y1 = lax.optimization_barrier((both_cores(others), from_y1))
    q = product(
        (1, 3),
        {
            "y1": [("A", 1, d) for d in range(4)],
            "y3": [("A", 3, d) for d in range(4)],
            "z1": [("B", 1, 2), ("B", 1, 1), ("B", 1, 1)],
            "z3": [("B", 3, 2), ("B", 3, 3), ("B", 3, 3)],
            "z1_last": [("B", 3, 1)],
            "z3_last": [("B", 1, 3)],
            "b": [("B", 1, 0), ("B", 3, 0)],
        },
        spots,
        masks,
        (others,),
        right,
        "second",
    )
    sum_y1 = along_y(join(q["y1"], 1, from_y3, "join_a"), 1)
    sum_y3 = along_y(join(q["y3"], 0, from_y1, "join_a"), 3)
    next_z1 = along_z(join(q["z1"], 2, from_z3, "join_b", p["z1_kept"]), 1)
    next_z3 = along_z(join(q["z3"], 2, from_z1, "join_b", p["z3_kept"]), 3)
    last_z1 = along_z(join(q["z1_last"], 0, next_z3, "join_b"), 1)
    last_z3 = along_z(join(q["z3_last"], 0, next_z1, "join_b"), 3)
    a = [a_own[d] + sum_y1[d] + sum_y3[d] for d in range(4)]
    b = [
        p["b"][0] + from_z1[1] + next_z3[2],
        q["b"][0] + next_z1[1] + last_z3[0],
        p["b"][1] + next_z1[2] + from_z3[1],
        q["b"][1] + last_z1[0] + next_z3[1],
    ]
    return total(
        [a[0], along_z(a[1], 1), along_z(a[3], 3), along_z(a[2], 2)],
        [b[0], along_y(b[1], 1), along_y(b[2], 2), along_y(b[3], 3)],
    )


def solution(mesh):
    torus = Mesh(mesh.devices.reshape(SIZES), AXES)
    in_specs = (
        P("yl", ("yh", "z", "x", "c")),
        P(("yh", "z", "yl"), ("x", "c")),
        P(),
        P(),
        P(),
    )
    return jax.shard_map(
        shards, mesh=torus, in_specs=in_specs, out_specs=P("yl", ("x", "c", "yh", "z")), check_vma=False
    )
```

profile of v0, /device:TPU:0, one launch (start us, length us, event | category | flops | bytes accessed | tf_op | source)
XLA Modules:
  0.0 89.9 jit_solution(5039342159105985297)
XLA Ops:
  0.0 3.1 %collective-permute-start.2 = (f32[512,128]{1,0:T(8,128)}, f32[512,128]{1,0:T(8,128)S(1)}, u32[]{:S(2)}, u32[]{:S(2)}) collective-permute-start(f32[512,128]{1,0:T(8,128)} %param.5), channel_id=1, source_target_pairs={{0,32},{1,33},{2,34},{3,35},{4,36},{5,37},{6,38},{7,39},{8,40},{9,... | collective-permute-start | bytes 786440 | tf_op jit(solution)/shard_map/ppermute | solution.py:21
  6.4 2.2 %shard_map.55 = (bf16[8,512,256]{2,1,0:T(8,128)(2,1)S(1)}, bf16[8,512,256]{2,1,0:T(8,128)(2,1)S(1)}) custom-call(s32[5]{0:T(128)S(1)} %stack.42.spots.refs_0_, s32[2,16]{1,0:T(2,128)S(1)} %copy-done.4, s32[16,32]{1,0:T(8,128)S(1)} %copy-done.2, s32[2,32]{1,0:T(2,128)S(1)} %copy-done.6, f32[512,2048]{1,0:T(8,128)} %right.1), custom_call_target="tpu_custom_call" | custom-call | flops 1 | bytes 1 | tf_op jit(solution)/shard_map/pallas_call | solution.py:72
  8.6 1.3 %copy-done = bf16[8,512,256]{2,1,0:T(8,128)(2,1)} copy-done((bf16[8,512,256]{2,1,0:T(8,128)(2,1)}, bf16[8,512,256]{2,1,0:T(8,128)(2,1)S(1)}, u32[]{:S(2)}) %copy-start) | copy-done | bytes 2097176
  9.9 1.0 %collective-permute-done.2 = f32[512,128]{1,0:T(8,128)S(1)} collective-permute-done((f32[512,128]{1,0:T(8,128)}, f32[512,128]{1,0:T(8,128)S(1)}, u32[]{:S(2)}, u32[]{:S(2)}) %collective-permute-start.2) | collective-permute-done | bytes 262176 | tf_op jit(solution)/shard_map/ppermute | solution.py:21
  11.0 4.6 %collective-permute-done.1 = f32[512,128]{1,0:T(8,128)S(1)} collective-permute-done((f32[512,128]{1,0:T(8,128)}, f32[512,128]{1,0:T(8,128)S(1)}, u32[]{:S(2)}, u32[]{:S(2)}) %collective-permute-start.1) | collective-permute-done | bytes 262176 | tf_op jit(solution)/shard_map/ppermute | solution.py:21
  15.8 1.7 %collective-permute-start.3 = (f32[2,512,128]{2,1,0:T(8,128)S(1)}, f32[2,512,128]{2,1,0:T(8,128)S(1)}, u32[]{:S(2)}, u32[]{:S(2)}) collective-permute-start(f32[2,512,128]{2,1,0:T(8,128)S(1)} %pad_maximum_fusion), channel_id=1, source_target_pairs={{0,64},{1,65},{2,66},{3,67},{4,68},{5,69},{6,70},{7,71},{8,72},{9,... | collective-permute-start | bytes 1572872 | tf_op jit(solution)/shard_map/ppermute | solution.py:21
  17.7 1.4 %shard_map.56 = (f32[1,256,256]{2,1,0:T(8,128)S(1)}, f32[3,256,256]{2,1,0:T(8,128)S(1)}, f32[2,256,256]{2,1,0:T(8,128)S(1)}, f32[2,256,256]{2,1,0:T(8,128)S(1)},...) custom-call(s32[5]{0:T(128)S(1)} %stack.42.spots.refs_0_, ...), custom_call_target="tpu_custom_call" | custom-call | flops 1 | bytes 1 | tf_op jit(solution)/shard_map/pallas_call | solution.py:142
  19.1 4.1 %collective-permute-start.14 = (f32[2,256,256]{2,1,0:T(8,128)S(1)}, f32[2,256,256]{2,1,0:T(8,128)S(1)}, u32[]{:S(2)}, u32[]{:S(2)}) collective-permute-start(f32[2,256,256]{2,1,0:T(8,128)S(1)} %get-tuple-element.49), channel_id=1, source_target_pairs={{0,3},{1,2},{2,1},{3,0},{4,7},{5,6},{6,5},{7,4},{8,11},{9,10},{10,... | collective-permute-start | bytes 1572872 | tf_op jit(solution)/shard_map/ppermute | solution.py:21
  23.2 3.9 %collective-permute-start.6 = (f32[3,256,256]{2,1,0:T(8,128)S(1)}, f32[3,256,256]{2,1,0:T(8,128)S(1)}, u32[]{:S(2)}, u32[]{:S(2)}) collective-permute-start(f32[3,256,256]{2,1,0:T(8,128)S(1)} %get-tuple-element.40), channel_id=1, source_target_pairs={{0,68},{1,69},{2,70},{3,71},{4,64},{5,65},{6,66},{7,67},{8,76},{9,... | collective-permute-start | bytes 2359304 | tf_op jit(solution)/shard_map/ppermute | solution.py:21
  27.2 3.4 %collective-permute-done.3 = f32[2,512,128]{2,1,0:T(8,128)S(1)} collective-permute-done((f32[2,512,128]{2,1,0:T(8,128)S(1)}, f32[2,512,128]{2,1,0:T(8,128)S(1)}, u32[]{:S(2)}, u32[]{:S(2)}) %collective-permute-start.3) | collective-permute-done | bytes 524320 | tf_op jit(solution)/shard_map/ppermute | solution.py:21
  30.7 4.6 %all_to_all.5.refs_4_ = f32[2,2,512,128]{3,2,1,0:T(8,128)S(1)} all-to-all(f32[2,2,512,128]{3,2,1,0:T(8,128)S(1)} %broadcast_in_dim.2), channel_id=1, replica_groups=mesh['yl'=2,'x'=4,'c'=2,'yh'=2,'z'=4] {'c'}, dimensions={0} | all-to-all | bytes 2097152 | tf_op jit(solution)/shard_map/all_to_all | solution.py:187
  35.8 2.4 %shard_map.57 = (f32[4,256,256]{2,1,0:T(8,128)S(1)}, f32[4,256,256]{2,1,0:T(8,128)S(1)}, f32[3,256,256]{2,1,0:T(8,128)S(1)}, f32[3,256,256]{2,1,0:T(8,128)S(1)},...) custom-call(s32[5]{0:T(128)S(1)} %stack.42.spots.refs_0_, ...), custom_call_target="tpu_custom_call" | custom-call | flops 1 | bytes 1 | tf_op jit(solution)/shard_map/pallas_call | solution.py:142
  39.3 3.3 %collective-permute-start.13 = (f32[3,256,256]{2,1,0:T(8,128)S(1)}, f32[3,256,256]{2,1,0:T(8,128)S(1)}, u32[]{:S(2)}, u32[]{:S(2)}) collective-permute-start(f32[3,256,256]{2,1,0:T(8,128)S(1)} %shard_map.60), channel_id=1, source_target_pairs={{0,3},{1,2},{2,1},{3,0},{4,7},{5,6},{6,5},{7,4},{8,11},{9,10},{10,... | collective-permute-start | bytes 2359304 | tf_op jit(solution)/shard_map/ppermute | solution.py:21
  42.6 3.3 %collective-permute-start.8 = (f32[4,256,256]{2,1,0:T(8,128)S(1)}, f32[4,256,256]{2,1,0:T(8,128)S(1)}, u32[]{:S(2)}, u32[]{:S(2)}) collective-permute-start(f32[4,256,256]{2,1,0:T(8,128)S(1)} %shard_map.59), channel_id=1, source_target_pairs={{0,68},{1,69},{2,70},{3,71},{4,64},{5,65},{6,66},{7,67},{8,76},{9,... | collective-permute-start | bytes 3145736 | tf_op jit(solution)/shard_map/ppermute | solution.py:21
  46.6 11.4 %collective-permute-done.15.arrived_ref = f32[3,256,256]{2,1,0:T(8,128)S(1)} collective-permute-done((f32[3,256,256]{2,1,0:T(8,128)S(1)}, f32[3,256,256]{2,1,0:T(8,128)S(1)}, u32[]{:S(2)}, u32[]{:S(2)}) %collective-permute-start.15) | collective-permute-done | bytes 786464 | tf_op jit(solution)/shard_map/ppermute | solution.py:21
  58.1 2.6 %collective-permute-start.16 = (f32[1,256,256]{2,1,0:T(8,128)S(1)}, f32[1,256,256]{2,1,0:T(8,128)S(1)}, u32[]{:S(2)}, u32[]{:S(2)}) collective-permute-start(f32[1,256,256]{2,1,0:T(8,128)S(1)} %shard_map.62), channel_id=1, source_target_pairs={{0,3},{1,2},{2,1},{3,0},{4,7},{5,6},{6,5},{7,4},{8,11},{9,10},{10,... | collective-permute-start | bytes 786440 | tf_op jit(solution)/shard_map/ppermute | solution.py:21
  60.6 1.0 %collective-permute-start.19 = (f32[1,256,256]{2,1,0:T(8,128)S(1)}, f32[1,256,256]{2,1,0:T(8,128)S(1)}, u32[]{:S(2)}, u32[]{:S(2)}) collective-permute-start(f32[1,256,256]{2,1,0:T(8,128)S(1)} %shard_map.63), channel_id=1, source_target_pairs={{0,1},{1,0},{2,3},{3,2},{4,5},{5,4},{6,7},{7,6},{8,9},{9,8},{10,11... | collective-permute-start | bytes 786440 | tf_op jit(solution)/shard_map/ppermute | solution.py:21
  61.6 6.8 %collective-permute-done.16 = f32[1,256,256]{2,1,0:T(8,128)S(1)} collective-permute-done((f32[1,256,256]{2,1,0:T(8,128)S(1)}, f32[1,256,256]{2,1,0:T(8,128)S(1)}, u32[]{:S(2)}, u32[]{:S(2)}) %collective-permute-start.16) | collective-permute-done | bytes 262176 | tf_op jit(solution)/shard_map/ppermute | solution.py:21
  69.6 4.1 %collective-permute-start.18 = (f32[256,256]{1,0:T(8,128)S(1)}, f32[256,256]{1,0:T(8,128)S(1)}, u32[]{:S(2)}, u32[]{:S(2)}) collective-permute-start(f32[256,256]{1,0:T(8,128)S(1)} %get-tuple-element.59), channel_id=1, source_target_pairs={{0,4},{1,5},{2,6},{3,7},{4,0},{5,1},{6,2},{7,3},{8,12},{9,13},{10,... | collective-permute-start | bytes 786440 | tf_op jit(solution)/shard_map/ppermute | solution.py:21
  74.6 2.2 %collective-permute-start.11 = (f32[256,256]{1,0:T(8,128)S(1)}, f32[256,256]{1,0:T(8,128)S(1)}, u32[]{:S(2)}, u32[]{:S(2)}) collective-permute-start(f32[256,256]{1,0:T(8,128)S(1)} %get-tuple-element.53), channel_id=1, source_target_pairs={{0,2},{1,3},{2,0},{3,1},{4,6},{5,7},{6,4},{7,5},{8,10},{9,11},{10,... | collective-permute-start | bytes 786440 | tf_op jit(solution)/shard_map/ppermute | solution.py:21
  76.9 1.1 %collective-permute-start.10 = (f32[256,256]{1,0:T(8,128)S(1)}, f32[256,256]{1,0:T(8,128)S(1)}, u32[]{:S(2)}, u32[]{:S(2)}) collective-permute-start(f32[256,256]{1,0:T(8,128)S(1)} %get-tuple-element.54), channel_id=1, source_target_pairs={{0,3},{1,2},{2,1},{3,0},{4,7},{5,6},{6,5},{7,4},{8,11},{9,10},{10,... | collective-permute-start | bytes 786440 | tf_op jit(solution)/shard_map/ppermute | solution.py:21
  78.0 2.9 %collective-permute-done.18.refs_6_ = f32[256,256]{1,0:T(8,128)S(1)} collective-permute-done((f32[256,256]{1,0:T(8,128)S(1)}, f32[256,256]{1,0:T(8,128)S(1)}, u32[]{:S(2)}, u32[]{:S(2)}) %collective-permute-start.18) | collective-permute-done | bytes 262176 | tf_op jit(solution)/shard_map/ppermute | solution.py:21
  81.6 2.9 %collective-permute-done.17.refs_5_ = f32[256,256]{1,0:T(8,128)S(1)} collective-permute-done((f32[256,256]{1,0:T(8,128)S(1)}, f32[256,256]{1,0:T(8,128)S(1)}, u32[]{:S(2)}, u32[]{:S(2)}) %collective-permute-start.17) | collective-permute-done | bytes 262176 | tf_op jit(solution)/shard_map/ppermute | solution.py:21
  85.1 3.6 %collective-permute-done.10.refs_2_ = f32[256,256]{1,0:T(8,128)S(1)} collective-permute-done((f32[256,256]{1,0:T(8,128)S(1)}, f32[256,256]{1,0:T(8,128)S(1)}, u32[]{:S(2)}, u32[]{:S(2)}) %collective-permute-start.10) | collective-permute-done | bytes 262176 | tf_op jit(solution)/shard_map/ppermute | solution.py:21
  (55 shorter events, 10.7 us)
Async XLA Ops:
  0.0 10.9 %collective-permute-start.2 = (f32[512,128]{1,0:T(8,128)}, f32[512,128]{1,0:T(8,128)S(1)}, u32[]{:S(2)}, u32[]{:S(2)}) collective-permute-start(f32[512,128]{1,0:T(8,128)} %param.5), channel_id=1, source_target_pairs={{0,32},{1,33},{2,34},{3,35},{4,36},{5,37},{6,38},{7,39},{8,40},{9,... | collective-permute-start | bytes 786440 | tf_op jit(solution)/shard_map/ppermute | solution.py:21
  3.1 12.5 %collective-permute-start.1 = (f32[512,128]{1,0:T(8,128)}, f32[512,128]{1,0:T(8,128)S(1)}, u32[]{:S(2)}, u32[]{:S(2)}) collective-permute-start(f32[512,128]{1,0:T(8,128)} %param.5), channel_id=1, source_target_pairs={{0,16},{1,17},{2,18},{3,19},{4,20},{5,21},{6,22},{7,23},{8,24},{9,... | collective-permute-start | bytes 786440 | tf_op jit(solution)/shard_map/ppermute | solution.py:21
  3.7 11.9 %collective-permute-start = (f32[512,128]{1,0:T(8,128)}, f32[512,128]{1,0:T(8,128)S(1)}, u32[]{:S(2)}, u32[]{:S(2)}) collective-permute-start(f32[512,128]{1,0:T(8,128)} %param.5), channel_id=1, source_target_pairs={{0,48},{1,49},{2,50},{3,51},{4,52},{5,53},{6,54},{7,55},{8,56},{9,... | collective-permute-start | bytes 786440 | tf_op jit(solution)/shard_map/ppermute | solution.py:21
  10.9 6.7 %copy-start.1 = (bf16[8,512,256]{2,1,0:T(8,128)(2,1)S(1)}, bf16[8,512,256]{2,1,0:T(8,128)(2,1)}, u32[]{:S(2)}) copy-start(bf16[8,512,256]{2,1,0:T(8,128)(2,1)} %copy-done) | copy-start | bytes 6291460
  10.9 6.7 %copy-start.3 = (s32[16,32]{1,0:T(8,128)S(1)}, s32[16,32]{1,0:T(8,128)}, u32[]{:S(2)}) copy-start(s32[16,32]{1,0:T(8,128)} %refs_2_.3) | copy-start | bytes 6148
  10.9 6.7 %copy-start.5 = (s32[2,16]{1,0:T(2,128)S(1)}, s32[2,16]{1,0:T(2,128)}, u32[]{:S(2)}) copy-start(s32[2,16]{1,0:T(2,128)} %refs_1_.3) | copy-start | bytes 388
  15.7 2.0 %collective-permute-start.4 = (f32[2,512,128]{2,1,0:T(8,128)S(1)}, f32[2,512,128]{2,1,0:T(8,128)S(1)}, u32[]{:S(2)}, u32[]{:S(2)}) collective-permute-start(f32[2,512,128]{2,1,0:T(8,128)S(1)} %pad_maximum_fusion.1.refs_4_), channel_id=1, source_target_pairs={{0,8},{1,9},{2,10},{3,11},{4,12},{5,13},{6,14},{7,15},{8,0},{9,1},... | collective-permute-start | bytes 1572872 | tf_op jit(solution)/shard_map/ppermute | solution.py:21
  15.8 14.8 %collective-permute-start.3 = (f32[2,512,128]{2,1,0:T(8,128)S(1)}, f32[2,512,128]{2,1,0:T(8,128)S(1)}, u32[]{:S(2)}, u32[]{:S(2)}) collective-permute-start(f32[2,512,128]{2,1,0:T(8,128)S(1)} %pad_maximum_fusion), channel_id=1, source_target_pairs={{0,64},{1,65},{2,66},{3,67},{4,68},{5,69},{6,70},{7,71},{8,72},{9,... | collective-permute-start | bytes 1572872 | tf_op jit(solution)/shard_map/ppermute | solution.py:21
  19.1 19.2 %collective-permute-start.14 = (f32[2,256,256]{2,1,0:T(8,128)S(1)}, f32[2,256,256]{2,1,0:T(8,128)S(1)}, u32[]{:S(2)}, u32[]{:S(2)}) collective-permute-start(f32[2,256,256]{2,1,0:T(8,128)S(1)} %get-tuple-element.49), channel_id=1, source_target_pairs={{0,3},{1,2},{2,1},{3,0},{4,7},{5,6},{6,5},{7,4},{8,11},{9,10},{10,... | collective-permute-start | bytes 1572872 | tf_op jit(solution)/shard_map/ppermute | solution.py:21
  23.2 16.0 %collective-permute-start.12 = (f32[2,256,256]{2,1,0:T(8,128)S(1)}, f32[2,256,256]{2,1,0:T(8,128)S(1)}, u32[]{:S(2)}, u32[]{:S(2)}) collective-permute-start(f32[2,256,256]{2,1,0:T(8,128)S(1)} %get-tuple-element.44), channel_id=1, source_target_pairs={{0,1},{1,0},{2,3},{3,2},{4,5},{5,4},{6,7},{7,6},{8,9},{9,8},{10,11... | collective-permute-start | bytes 1572872 | tf_op jit(solution)/shard_map/ppermute | solution.py:21
  23.2 22.7 %collective-permute-start.6 = (f32[3,256,256]{2,1,0:T(8,128)S(1)}, f32[3,256,256]{2,1,0:T(8,128)S(1)}, u32[]{:S(2)}, u32[]{:S(2)}) collective-permute-start(f32[3,256,256]{2,1,0:T(8,128)S(1)} %get-tuple-element.40), channel_id=1, source_target_pairs={{0,68},{1,69},{2,70},{3,71},{4,64},{5,65},{6,66},{7,67},{8,76},{9,... | collective-permute-start | bytes 2359304 | tf_op jit(solution)/shard_map/ppermute | solution.py:21
  27.1 8.7 %collective-permute-start.5 = (f32[1,256,256]{2,1,0:T(8,128)S(1)}, f32[1,256,256]{2,1,0:T(8,128)S(1)}, u32[]{:S(2)}, u32[]{:S(2)}) collective-permute-start(f32[1,256,256]{2,1,0:T(8,128)S(1)} %get-tuple-element.37), channel_id=1, source_target_pairs={{0,64},{1,65},{2,66},{3,67},{4,68},{5,69},{6,70},{7,71},{8,72},{9,... | collective-permute-start | bytes 786440 | tf_op jit(solution)/shard_map/ppermute | solution.py:21
  38.3 19.7 %collective-permute-start.15 = (f32[3,256,256]{2,1,0:T(8,128)S(1)}, f32[3,256,256]{2,1,0:T(8,128)S(1)}, u32[]{:S(2)}, u32[]{:S(2)}) collective-permute-start(f32[3,256,256]{2,1,0:T(8,128)S(1)} %shard_map.61), channel_id=1, source_target_pairs={{0,1},{1,0},{2,3},{3,2},{4,5},{5,4},{6,7},{7,6},{8,9},{9,8},{10,11... | collective-permute-start | bytes 2359304 | tf_op jit(solution)/shard_map/ppermute | solution.py:21
  39.3 21.4 %collective-permute-start.13 = (f32[3,256,256]{2,1,0:T(8,128)S(1)}, f32[3,256,256]{2,1,0:T(8,128)S(1)}, u32[]{:S(2)}, u32[]{:S(2)}) collective-permute-start(f32[3,256,256]{2,1,0:T(8,128)S(1)} %shard_map.60), channel_id=1, source_target_pairs={{0,3},{1,2},{2,1},{3,0},{4,7},{5,6},{6,5},{7,4},{8,11},{9,10},{10,... | collective-permute-start | bytes 2359304 | tf_op jit(solution)/shard_map/ppermute | solution.py:21
  42.6 31.8 %collective-permute-start.8 = (f32[4,256,256]{2,1,0:T(8,128)S(1)}, f32[4,256,256]{2,1,0:T(8,128)S(1)}, u32[]{:S(2)}, u32[]{:S(2)}) collective-permute-start(f32[4,256,256]{2,1,0:T(8,128)S(1)} %shard_map.59), channel_id=1, source_target_pairs={{0,68},{1,69},{2,70},{3,71},{4,64},{5,65},{6,66},{7,67},{8,76},{9,... | collective-permute-start | bytes 3145736 | tf_op jit(solution)/shard_map/ppermute | solution.py:21
  46.0 28.4 %collective-permute-start.7 = (f32[4,256,256]{2,1,0:T(8,128)S(1)}, f32[4,256,256]{2,1,0:T(8,128)S(1)}, u32[]{:S(2)}, u32[]{:S(2)}) collective-permute-start(f32[4,256,256]{2,1,0:T(8,128)S(1)} %shard_map.58), channel_id=1, source_target_pairs={{0,64},{1,65},{2,66},{3,67},{4,68},{5,69},{6,70},{7,71},{8,72},{9,... | collective-permute-start | bytes 3145736 | tf_op jit(solution)/shard_map/ppermute | solution.py:21
  58.1 10.4 %collective-permute-start.16 = (f32[1,256,256]{2,1,0:T(8,128)S(1)}, f32[1,256,256]{2,1,0:T(8,128)S(1)}, u32[]{:S(2)}, u32[]{:S(2)}) collective-permute-start(f32[1,256,256]{2,1,0:T(8,128)S(1)} %shard_map.62), channel_id=1, source_target_pairs={{0,3},{1,2},{2,1},{3,0},{4,7},{5,6},{6,5},{7,4},{8,11},{9,10},{10,... | collective-permute-start | bytes 786440 | tf_op jit(solution)/shard_map/ppermute | solution.py:21
  60.6 8.8 %collective-permute-start.19 = (f32[1,256,256]{2,1,0:T(8,128)S(1)}, f32[1,256,256]{2,1,0:T(8,128)S(1)}, u32[]{:S(2)}, u32[]{:S(2)}) collective-permute-start(f32[1,256,256]{2,1,0:T(8,128)S(1)} %shard_map.63), channel_id=1, source_target_pairs={{0,1},{1,0},{2,3},{3,2},{4,5},{5,4},{6,7},{7,6},{8,9},{9,8},{10,11... | collective-permute-start | bytes 786440 | tf_op jit(solution)/shard_map/ppermute | solution.py:21
  69.6 11.4 %collective-permute-start.18 = (f32[256,256]{1,0:T(8,128)S(1)}, f32[256,256]{1,0:T(8,128)S(1)}, u32[]{:S(2)}, u32[]{:S(2)}) collective-permute-start(f32[256,256]{1,0:T(8,128)S(1)} %get-tuple-element.59), channel_id=1, source_target_pairs={{0,4},{1,5},{2,6},{3,7},{4,0},{5,1},{6,2},{7,3},{8,12},{9,13},{10,... | collective-permute-start | bytes 786440 | tf_op jit(solution)/shard_map/ppermute | solution.py:21
  73.8 10.7 %collective-permute-start.17 = (f32[256,256]{1,0:T(8,128)S(1)}, f32[256,256]{1,0:T(8,128)S(1)}, u32[]{:S(2)}, u32[]{:S(2)}) collective-permute-start(f32[256,256]{1,0:T(8,128)S(1)} %get-tuple-element.60), channel_id=1, source_target_pairs={{0,64},{1,65},{2,66},{3,67},{4,68},{5,69},{6,70},{7,71},{8,72},{9,... | collective-permute-start | bytes 786440 | tf_op jit(solution)/shard_map/ppermute | solution.py:21
  73.8 11.4 %collective-permute-start.20 = (f32[256,256]{1,0:T(8,128)S(1)}, f32[256,256]{1,0:T(8,128)S(1)}, u32[]{:S(2)}, u32[]{:S(2)}) collective-permute-start(f32[256,256]{1,0:T(8,128)S(1)} %get-tuple-element.62), channel_id=1, source_target_pairs={{0,68},{1,69},{2,70},{3,71},{4,64},{5,65},{6,66},{7,67},{8,76},{9,... | collective-permute-start | bytes 786440 | tf_op jit(solution)/shard_map/ppermute | solution.py:21
  74.6 10.5 %collective-permute-start.11 = (f32[256,256]{1,0:T(8,128)S(1)}, f32[256,256]{1,0:T(8,128)S(1)}, u32[]{:S(2)}, u32[]{:S(2)}) collective-permute-start(f32[256,256]{1,0:T(8,128)S(1)} %get-tuple-element.53), channel_id=1, source_target_pairs={{0,2},{1,3},{2,0},{3,1},{4,6},{5,7},{6,4},{7,5},{8,10},{9,11},{10,... | collective-permute-start | bytes 786440 | tf_op jit(solution)/shard_map/ppermute | solution.py:21
  76.9 11.9 %collective-permute-start.10 = (f32[256,256]{1,0:T(8,128)S(1)}, f32[256,256]{1,0:T(8,128)S(1)}, u32[]{:S(2)}, u32[]{:S(2)}) collective-permute-start(f32[256,256]{1,0:T(8,128)S(1)} %get-tuple-element.54), channel_id=1, source_target_pairs={{0,3},{1,2},{2,1},{3,0},{4,7},{5,6},{6,5},{7,4},{8,11},{9,10},{10,... | collective-permute-start | bytes 786440 | tf_op jit(solution)/shard_map/ppermute | solution.py:21
  81.0 8.0 %collective-permute-start.9 = (f32[256,256]{1,0:T(8,128)S(1)}, f32[256,256]{1,0:T(8,128)S(1)}, u32[]{:S(2)}, u32[]{:S(2)}) collective-permute-start(f32[256,256]{1,0:T(8,128)S(1)} %get-tuple-element.55), channel_id=1, source_target_pairs={{0,1},{1,0},{2,3},{3,2},{4,5},{5,4},{6,7},{7,6},{8,9},{9,8},{10,11... | collective-permute-start | bytes 786440 | tf_op jit(solution)/shard_map/ppermute | solution.py:21
  (6 other events, 14.7 us)
where the time goes:
time: 89.9 us
  waiting for transfers between devices  39.3 us (44%)
  starting transfers between devices  34.5 us (38%)
  Pallas kernels  7.18 us (8%)
  blocking collectives  4.58 us (5%)
  local copies, waits for them, and re-layouts  3.56 us (4%)
    ppermute x21, waiting for transfers between devices, permute(): return lax.ppermute(value, AXES, [(n, n ^ bits) for n in range(128)])  39.3 us
    ppermute x21, starting transfers between devices, permute(): return lax.ppermute(value, AXES, [(n, n ^ bits) for n in range(128)])  34.5 us
    all_to_all x1, blocking collectives, both_cores(): lax.all_to_all(jnp.broadcast_to(value[None], (2, *value.shape)), 'c', 0,...  4.58 us
    pallas_call x2, Pallas kernels, product(): pl.pallas_call(lambda *refs: product_kernel(turns, plan, len(pieces), *re...  3.8 us
    unnamed x18, local copies, waits for them, and re-layouts  3.41 us
    pallas_call x1, Pallas kernels, split(): pl.pallas_call(split_kernel, out_shape=[jax.ShapeDtypeStruct((8, TILE, WI...  2.17 us
  transfers between devices with their start and end apart: 21, of which 13 were waited for; matrix products, arithmetic and copies ran while one was open for 1% of the time, Pallas kernels for 7%

commit v1 on v0

--- a/solution.py
+++ b/solution.py
@@ -195,7 +195,6 @@
     here = x // 2 == yl
     across, beside, between = (permute(left, x=bits) for bits in (2, 3, 1))
     right = split(spots, masks, right)
-    across, right = lax.optimization_barrier((across, right))
     mine = jnp.stack([jnp.where(here, between, beside), jnp.where(here, left, across)])
     others = jnp.stack([jnp.where(here, beside, between), jnp.where(here, across, left)])
     others = along_y(others, 1)

time: 89.9 us -> 91.1 us (1.013)
  the two profiles are of different devices: /device:TPU:0 before, /device:TPU:5 now
where the time goes in v1:
time: 91.1 us; the launch traced here: 90.8 us
  waiting for transfers between devices  48.3 us (53%)
  starting transfers between devices  26 us (29%)
  Pallas kernels  9.59 us (11%)
  blocking collectives  5.01 us (5%)
  other arithmetic  1.53 us (2%)
    ppermute x21, waiting for transfers between devices, permute(): return lax.ppermute(value, AXES, [(n, n ^ bits) for n in range(128)])  48.3 us
    ppermute x21, starting transfers between devices, permute(): return lax.ppermute(value, AXES, [(n, n ^ bits) for n in range(128)])  26 us
    pallas_call x2, Pallas kernels, product(): pl.pallas_call(lambda *refs: product_kernel(turns, plan, len(pieces), *re...  5.93 us
    all_to_all x1, blocking collectives, both_cores(): lax.all_to_all(jnp.broadcast_to(value[None], (2, *value.shape)), 'c', 0,...  5.01 us
    pallas_call x1, Pallas kernels, split(): pl.pallas_call(split_kernel, out_shape=[jax.ShapeDtypeStruct((8, TILE, WI...  2.47 us
  transfers between devices with their start and end apart: 21, of which 14 were waited for; matrix products, arithmetic and copies ran while one was open for 2% of the time, Pallas kernels for 10%

profile of v1, /device:TPU:5, one launch (start us, length us, event | category | flops | bytes accessed | tf_op | source)
XLA Modules:
  0.0 90.8 jit_solution(2257990308157557029)
XLA Ops:
  0.0 2.0 %collective-permute-start.1 = (f32[512,128]{1,0:T(8,128)}, f32[512,128]{1,0:T(8,128)S(1)}, u32[]{:S(2)}, u32[]{:S(2)}) collective-permute-start(f32[512,128]{1,0:T(8,128)} %param.5), channel_id=1, source_target_pairs={{0,16},{1,17},{2,18},{3,19},{4,20},{5,21},{6,22},{7,23},{8,24},{9,... | collective-permute-start | bytes 786440 | tf_op jit(solution)/shard_map/ppermute | solution.py:21
  3.3 5.7 %collective-permute-done.2 = f32[512,128]{1,0:T(8,128)S(1)} collective-permute-done((f32[512,128]{1,0:T(8,128)}, f32[512,128]{1,0:T(8,128)S(1)}, u32[]{:S(2)}, u32[]{:S(2)}) %collective-permute-start.2) | collective-permute-done | bytes 262176 | tf_op jit(solution)/shard_map/ppermute | solution.py:21
  9.9 3.7 %collective-permute-done.1 = f32[512,128]{1,0:T(8,128)S(1)} collective-permute-done((f32[512,128]{1,0:T(8,128)}, f32[512,128]{1,0:T(8,128)S(1)}, u32[]{:S(2)}, u32[]{:S(2)}) %collective-permute-start.1) | collective-permute-done | bytes 262176 | tf_op jit(solution)/shard_map/ppermute | solution.py:21
  13.6 1.9 %collective-permute-done = f32[512,128]{1,0:T(8,128)S(1)} collective-permute-done((f32[512,128]{1,0:T(8,128)}, f32[512,128]{1,0:T(8,128)S(1)}, u32[]{:S(2)}, u32[]{:S(2)}) %collective-permute-start) | collective-permute-done | bytes 262176 | tf_op jit(solution)/shard_map/ppermute | solution.py:21
  16.3 1.4 %collective-permute-start.3 = (f32[2,512,128]{2,1,0:T(8,128)S(1)}, f32[2,512,128]{2,1,0:T(8,128)S(1)}, u32[]{:S(2)}, u32[]{:S(2)}) collective-permute-start(f32[2,512,128]{2,1,0:T(8,128)S(1)} %pad_maximum_fusion), channel_id=1, source_target_pairs={{0,64},{1,65},{2,66},{3,67},{4,68},{5,69},{6,70},{7,71},{8,72},{9,... | collective-permute-start | bytes 1572872 | tf_op jit(solution)/shard_map/ppermute | solution.py:21
  17.7 2.5 %shard_map.55 = (bf16[8,512,256]{2,1,0:T(8,128)(2,1)S(1)}, bf16[8,512,256]{2,1,0:T(8,128)(2,1)S(1)}) custom-call(s32[5]{0:T(128)S(1)} %stack.44.spots.refs_0_, s32[2,16]{1,0:T(2,128)S(1)} %copy-done.1, s32[16,32]{1,0:T(8,128)S(1)} %copy-done, s32[2,32]{1,0:T(2,128)S(1)} %copy-done.2, f32[512,2048]{1,0:T(8,128)} %right.1), custom_call_target="tpu_custom_call" | custom-call | flops 1 | bytes 1 | tf_op jit(solution)/shard_map/pallas_call | solution.py:72
  20.2 3.5 %shard_map.56 = (f32[1,256,256]{2,1,0:T(8,128)S(1)}, f32[3,256,256]{2,1,0:T(8,128)S(1)}, f32[2,256,256]{2,1,0:T(8,128)S(1)}, f32[2,256,256]{2,1,0:T(8,128)S(1)},...) custom-call(s32[5]{0:T(128)S(1)} %stack.44.spots.refs_0_, ...), custom_call_target="tpu_custom_call" | custom-call | flops 1 | bytes 1 | tf_op jit(solution)/shard_map/pallas_call | solution.py:142
  23.7 2.5 %collective-permute-start.14 = (f32[2,256,256]{2,1,0:T(8,128)S(1)}, f32[2,256,256]{2,1,0:T(8,128)S(1)}, u32[]{:S(2)}, u32[]{:S(2)}) collective-permute-start(f32[2,256,256]{2,1,0:T(8,128)S(1)} %get-tuple-element.43), channel_id=1, source_target_pairs={{0,3},{1,2},{2,1},{3,0},{4,7},{5,6},{6,5},{7,4},{8,11},{9,10},{10,... | collective-permute-start | bytes 1572872 | tf_op jit(solution)/shard_map/ppermute | solution.py:21
  26.2 3.6 %collective-permute-start.6 = (f32[3,256,256]{2,1,0:T(8,128)S(1)}, f32[3,256,256]{2,1,0:T(8,128)S(1)}, u32[]{:S(2)}, u32[]{:S(2)}) collective-permute-start(f32[3,256,256]{2,1,0:T(8,128)S(1)} %get-tuple-element.34), channel_id=1, source_target_pairs={{0,68},{1,69},{2,70},{3,71},{4,64},{5,65},{6,66},{7,67},{8,76},{9,... | collective-permute-start | bytes 2359304 | tf_op jit(solution)/shard_map/ppermute | solution.py:21
  29.9 5.0 %all_to_all.5.refs_4_ = f32[2,2,512,128]{3,2,1,0:T(8,128)S(1)} all-to-all(f32[2,2,512,128]{3,2,1,0:T(8,128)S(1)} %broadcast_in_dim.2), channel_id=1, replica_groups=mesh['yl'=2,'x'=4,'c'=2,'yh'=2,'z'=4] {'c'}, dimensions={0} | all-to-all | bytes 2097152 | tf_op jit(solution)/shard_map/all_to_all | solution.py:187
  35.0 3.1 %collective-permute-done.5.arrived_ref = f32[1,256,256]{2,1,0:T(8,128)S(1)} collective-permute-done((f32[1,256,256]{2,1,0:T(8,128)S(1)}, f32[1,256,256]{2,1,0:T(8,128)S(1)}, u32[]{:S(2)}, u32[]{:S(2)}) %collective-permute-start.5) | collective-permute-done | bytes 262176 | tf_op jit(solution)/shard_map/ppermute | solution.py:21
  38.1 2.4 %shard_map.57 = (f32[4,256,256]{2,1,0:T(8,128)S(1)}, f32[4,256,256]{2,1,0:T(8,128)S(1)}, f32[3,256,256]{2,1,0:T(8,128)S(1)}, f32[3,256,256]{2,1,0:T(8,128)S(1)},...) custom-call(s32[5]{0:T(128)S(1)} %stack.44.spots.refs_0_, ...), custom_call_target="tpu_custom_call" | custom-call | flops 1 | bytes 1 | tf_op jit(solution)/shard_map/pallas_call | solution.py:142
  40.5 2.4 %collective-permute-start.15 = (f32[3,256,256]{2,1,0:T(8,128)S(1)}, f32[3,256,256]{2,1,0:T(8,128)S(1)}, u32[]{:S(2)}, u32[]{:S(2)}) collective-permute-start(f32[3,256,256]{2,1,0:T(8,128)S(1)} %shard_map.61), channel_id=1, source_target_pairs={{0,1},{1,0},{2,3},{3,2},{4,5},{5,4},{6,7},{7,6},{8,9},{9,8},{10,11... | collective-permute-start | bytes 2359304 | tf_op jit(solution)/shard_map/ppermute | solution.py:21
  43.5 2.5 %collective-permute-start.8 = (f32[4,256,256]{2,1,0:T(8,128)S(1)}, f32[4,256,256]{2,1,0:T(8,128)S(1)}, u32[]{:S(2)}, u32[]{:S(2)}) collective-permute-start(f32[4,256,256]{2,1,0:T(8,128)S(1)} %shard_map.59), channel_id=1, source_target_pairs={{0,68},{1,69},{2,70},{3,71},{4,64},{5,65},{6,66},{7,67},{8,76},{9,... | collective-permute-start | bytes 3145736 | tf_op jit(solution)/shard_map/ppermute | solution.py:21
  46.0 1.7 %collective-permute-done.6.arrived_ref = f32[3,256,256]{2,1,0:T(8,128)S(1)} collective-permute-done((f32[3,256,256]{2,1,0:T(8,128)S(1)}, f32[3,256,256]{2,1,0:T(8,128)S(1)}, u32[]{:S(2)}, u32[]{:S(2)}) %collective-permute-start.6) | collective-permute-done | bytes 786464 | tf_op jit(solution)/shard_map/ppermute | solution.py:21
  47.9 13.0 %collective-permute-done.15.arrived_ref = f32[3,256,256]{2,1,0:T(8,128)S(1)} collective-permute-done((f32[3,256,256]{2,1,0:T(8,128)S(1)}, f32[3,256,256]{2,1,0:T(8,128)S(1)}, u32[]{:S(2)}, u32[]{:S(2)}) %collective-permute-start.15) | collective-permute-done | bytes 786464 | tf_op jit(solution)/shard_map/ppermute | solution.py:21
  61.1 2.4 %collective-permute-done.13.arrived_ref = f32[3,256,256]{2,1,0:T(8,128)S(1)} collective-permute-done((f32[3,256,256]{2,1,0:T(8,128)S(1)}, f32[3,256,256]{2,1,0:T(8,128)S(1)}, u32[]{:S(2)}, u32[]{:S(2)}) %collective-permute-start.13) | collective-permute-done | bytes 786464 | tf_op jit(solution)/shard_map/ppermute | solution.py:21
  63.7 6.2 %collective-permute-done.16 = f32[1,256,256]{2,1,0:T(8,128)S(1)} collective-permute-done((f32[1,256,256]{2,1,0:T(8,128)S(1)}, f32[1,256,256]{2,1,0:T(8,128)S(1)}, u32[]{:S(2)}, u32[]{:S(2)}) %collective-permute-start.16) | collective-permute-done | bytes 262176 | tf_op jit(solution)/shard_map/ppermute | solution.py:21
  72.5 1.8 %collective-permute-start.20 = (f32[256,256]{1,0:T(8,128)S(1)}, f32[256,256]{1,0:T(8,128)S(1)}, u32[]{:S(2)}, u32[]{:S(2)}) collective-permute-start(f32[256,256]{1,0:T(8,128)S(1)} %get-tuple-element.56), channel_id=1, source_target_pairs={{0,68},{1,69},{2,70},{3,71},{4,64},{5,65},{6,66},{7,67},{8,76},{9,... | collective-permute-start | bytes 786440 | tf_op jit(solution)/shard_map/ppermute | solution.py:21
  75.5 1.9 %collective-permute-start.10 = (f32[256,256]{1,0:T(8,128)S(1)}, f32[256,256]{1,0:T(8,128)S(1)}, u32[]{:S(2)}, u32[]{:S(2)}) collective-permute-start(f32[256,256]{1,0:T(8,128)S(1)} %get-tuple-element.48), channel_id=1, source_target_pairs={{0,3},{1,2},{2,1},{3,0},{4,7},{5,6},{6,5},{7,4},{8,11},{9,10},{10,... | collective-permute-start | bytes 786440 | tf_op jit(solution)/shard_map/ppermute | solution.py:21
  77.4 1.5 %collective-permute-done.18.refs_6_ = f32[256,256]{1,0:T(8,128)S(1)} collective-permute-done((f32[256,256]{1,0:T(8,128)S(1)}, f32[256,256]{1,0:T(8,128)S(1)}, u32[]{:S(2)}, u32[]{:S(2)}) %collective-permute-start.18) | collective-permute-done | bytes 262176 | tf_op jit(solution)/shard_map/ppermute | solution.py:21
  78.9 2.9 %collective-permute-start.9 = (f32[256,256]{1,0:T(8,128)S(1)}, f32[256,256]{1,0:T(8,128)S(1)}, u32[]{:S(2)}, u32[]{:S(2)}) collective-permute-start(f32[256,256]{1,0:T(8,128)S(1)} %get-tuple-element.49), channel_id=1, source_target_pairs={{0,1},{1,0},{2,3},{3,2},{4,5},{5,4},{6,7},{7,6},{8,9},{9,8},{10,11... | collective-permute-start | bytes 786440 | tf_op jit(solution)/shard_map/ppermute | solution.py:21
  82.5 3.8 %collective-permute-done.20.refs_7_ = f32[256,256]{1,0:T(8,128)S(1)} collective-permute-done((f32[256,256]{1,0:T(8,128)S(1)}, f32[256,256]{1,0:T(8,128)S(1)}, u32[]{:S(2)}, u32[]{:S(2)}) %collective-permute-start.20) | collective-permute-done | bytes 262176 | tf_op jit(solution)/shard_map/ppermute | solution.py:21
  86.2 3.6 %collective-permute-done.10.refs_2_ = f32[256,256]{1,0:T(8,128)S(1)} collective-permute-done((f32[256,256]{1,0:T(8,128)S(1)}, f32[256,256]{1,0:T(8,128)S(1)}, u32[]{:S(2)}, u32[]{:S(2)}) %collective-permute-start.10) | collective-permute-done | bytes 262176 | tf_op jit(solution)/shard_map/ppermute | solution.py:21
  (43 shorter events, 9.6 us)
Async XLA Ops:
  0.0 8.9 %collective-permute-start.2 = (f32[512,128]{1,0:T(8,128)}, f32[512,128]{1,0:T(8,128)S(1)}, u32[]{:S(2)}, u32[]{:S(2)}) collective-permute-start(f32[512,128]{1,0:T(8,128)} %param.5), channel_id=1, source_target_pairs={{0,32},{1,33},{2,34},{3,35},{4,36},{5,37},{6,38},{7,39},{8,40},{9,... | collective-permute-start | bytes 786440 | tf_op jit(solution)/shard_map/ppermute | solution.py:21
  0.0 13.6 %collective-permute-start.1 = (f32[512,128]{1,0:T(8,128)}, f32[512,128]{1,0:T(8,128)S(1)}, u32[]{:S(2)}, u32[]{:S(2)}) collective-permute-start(f32[512,128]{1,0:T(8,128)} %param.5), channel_id=1, source_target_pairs={{0,16},{1,17},{2,18},{3,19},{4,20},{5,21},{6,22},{7,23},{8,24},{9,... | collective-permute-start | bytes 786440 | tf_op jit(solution)/shard_map/ppermute | solution.py:21
  2.0 13.5 %collective-permute-start = (f32[512,128]{1,0:T(8,128)}, f32[512,128]{1,0:T(8,128)S(1)}, u32[]{:S(2)}, u32[]{:S(2)}) collective-permute-start(f32[512,128]{1,0:T(8,128)} %param.5), channel_id=1, source_target_pairs={{0,48},{1,49},{2,50},{3,51},{4,52},{5,53},{6,54},{7,55},{8,56},{9,... | collective-permute-start | bytes 786440 | tf_op jit(solution)/shard_map/ppermute | solution.py:21
  3.3 14.5 %copy-start = (s32[16,32]{1,0:T(8,128)S(1)}, s32[16,32]{1,0:T(8,128)}, u32[]{:S(2)}) copy-start(s32[16,32]{1,0:T(8,128)} %refs_2_.3) | copy-start | bytes 6148
  3.3 14.5 %copy-start.1 = (s32[2,16]{1,0:T(2,128)S(1)}, s32[2,16]{1,0:T(2,128)}, u32[]{:S(2)}) copy-start(s32[2,16]{1,0:T(2,128)} %refs_1_.3) | copy-start | bytes 388
  3.3 14.5 %copy-start.2 = (s32[2,32]{1,0:T(2,128)S(1)}, s32[2,32]{1,0:T(2,128)}, u32[]{:S(2)}) copy-start(s32[2,32]{1,0:T(2,128)} %refs_3_.3) | copy-start | bytes 772
  15.6 4.6 %collective-permute-start.4 = (f32[2,512,128]{2,1,0:T(8,128)S(1)}, f32[2,512,128]{2,1,0:T(8,128)S(1)}, u32[]{:S(2)}, u32[]{:S(2)}) collective-permute-start(f32[2,512,128]{2,1,0:T(8,128)S(1)} %pad_maximum_fusion.1.refs_4_), channel_id=1, source_target_pairs={{0,8},{1,9},{2,10},{3,11},{4,12},{5,13},{6,14},{7,15},{8,0},{9,1},... | collective-permute-start | bytes 1572872 | tf_op jit(solution)/shard_map/ppermute | solution.py:21
  16.3 13.6 %collective-permute-start.3 = (f32[2,512,128]{2,1,0:T(8,128)S(1)}, f32[2,512,128]{2,1,0:T(8,128)S(1)}, u32[]{:S(2)}, u32[]{:S(2)}) collective-permute-start(f32[2,512,128]{2,1,0:T(8,128)S(1)} %pad_maximum_fusion), channel_id=1, source_target_pairs={{0,64},{1,65},{2,66},{3,67},{4,68},{5,69},{6,70},{7,71},{8,72},{9,... | collective-permute-start | bytes 1572872 | tf_op jit(solution)/shard_map/ppermute | solution.py:21
  23.7 16.7 %collective-permute-start.14 = (f32[2,256,256]{2,1,0:T(8,128)S(1)}, f32[2,256,256]{2,1,0:T(8,128)S(1)}, u32[]{:S(2)}, u32[]{:S(2)}) collective-permute-start(f32[2,256,256]{2,1,0:T(8,128)S(1)} %get-tuple-element.43), channel_id=1, source_target_pairs={{0,3},{1,2},{2,1},{3,0},{4,7},{5,6},{6,5},{7,4},{8,11},{9,10},{10,... | collective-permute-start | bytes 1572872 | tf_op jit(solution)/shard_map/ppermute | solution.py:21
  26.2 16.7 %collective-permute-start.12 = (f32[2,256,256]{2,1,0:T(8,128)S(1)}, f32[2,256,256]{2,1,0:T(8,128)S(1)}, u32[]{:S(2)}, u32[]{:S(2)}) collective-permute-start(f32[2,256,256]{2,1,0:T(8,128)S(1)} %get-tuple-element.38), channel_id=1, source_target_pairs={{0,1},{1,0},{2,3},{3,2},{4,5},{5,4},{6,7},{7,6},{8,9},{9,8},{10,11... | collective-permute-start | bytes 1572872 | tf_op jit(solution)/shard_map/ppermute | solution.py:21
  26.2 21.5 %collective-permute-start.6 = (f32[3,256,256]{2,1,0:T(8,128)S(1)}, f32[3,256,256]{2,1,0:T(8,128)S(1)}, u32[]{:S(2)}, u32[]{:S(2)}) collective-permute-start(f32[3,256,256]{2,1,0:T(8,128)S(1)} %get-tuple-element.34), channel_id=1, source_target_pairs={{0,68},{1,69},{2,70},{3,71},{4,64},{5,65},{6,66},{7,67},{8,76},{9,... | collective-permute-start | bytes 2359304 | tf_op jit(solution)/shard_map/ppermute | solution.py:21
  29.8 8.3 %collective-permute-start.5 = (f32[1,256,256]{2,1,0:T(8,128)S(1)}, f32[1,256,256]{2,1,0:T(8,128)S(1)}, u32[]{:S(2)}, u32[]{:S(2)}) collective-permute-start(f32[1,256,256]{2,1,0:T(8,128)S(1)} %get-tuple-element.31), channel_id=1, source_target_pairs={{0,64},{1,65},{2,66},{3,67},{4,68},{5,69},{6,70},{7,71},{8,72},{9,... | collective-permute-start | bytes 786440 | tf_op jit(solution)/shard_map/ppermute | solution.py:21
  40.5 20.4 %collective-permute-start.15 = (f32[3,256,256]{2,1,0:T(8,128)S(1)}, f32[3,256,256]{2,1,0:T(8,128)S(1)}, u32[]{:S(2)}, u32[]{:S(2)}) collective-permute-start(f32[3,256,256]{2,1,0:T(8,128)S(1)} %shard_map.61), channel_id=1, source_target_pairs={{0,1},{1,0},{2,3},{3,2},{4,5},{5,4},{6,7},{7,6},{8,9},{9,8},{10,11... | collective-permute-start | bytes 2359304 | tf_op jit(solution)/shard_map/ppermute | solution.py:21
  43.0 20.6 %collective-permute-start.13 = (f32[3,256,256]{2,1,0:T(8,128)S(1)}, f32[3,256,256]{2,1,0:T(8,128)S(1)}, u32[]{:S(2)}, u32[]{:S(2)}) collective-permute-start(f32[3,256,256]{2,1,0:T(8,128)S(1)} %shard_map.60), channel_id=1, source_target_pairs={{0,3},{1,2},{2,1},{3,0},{4,7},{5,6},{6,5},{7,4},{8,11},{9,10},{10,... | collective-permute-start | bytes 2359304 | tf_op jit(solution)/shard_map/ppermute | solution.py:21
  43.5 30.9 %collective-permute-start.8 = (f32[4,256,256]{2,1,0:T(8,128)S(1)}, f32[4,256,256]{2,1,0:T(8,128)S(1)}, u32[]{:S(2)}, u32[]{:S(2)}) collective-permute-start(f32[4,256,256]{2,1,0:T(8,128)S(1)} %shard_map.59), channel_id=1, source_target_pairs={{0,68},{1,69},{2,70},{3,71},{4,64},{5,65},{6,66},{7,67},{8,76},{9,... | collective-permute-start | bytes 3145736 | tf_op jit(solution)/shard_map/ppermute | solution.py:21
  47.8 26.6 %collective-permute-start.7 = (f32[4,256,256]{2,1,0:T(8,128)S(1)}, f32[4,256,256]{2,1,0:T(8,128)S(1)}, u32[]{:S(2)}, u32[]{:S(2)}) collective-permute-start(f32[4,256,256]{2,1,0:T(8,128)S(1)} %shard_map.58), channel_id=1, source_target_pairs={{0,64},{1,65},{2,66},{3,67},{4,68},{5,69},{6,70},{7,71},{8,72},{9,... | collective-permute-start | bytes 3145736 | tf_op jit(solution)/shard_map/ppermute | solution.py:21
  61.0 8.9 %collective-permute-start.16 = (f32[1,256,256]{2,1,0:T(8,128)S(1)}, f32[1,256,256]{2,1,0:T(8,128)S(1)}, u32[]{:S(2)}, u32[]{:S(2)}) collective-permute-start(f32[1,256,256]{2,1,0:T(8,128)S(1)} %shard_map.62), channel_id=1, source_target_pairs={{0,3},{1,2},{2,1},{3,0},{4,7},{5,6},{6,5},{7,4},{8,11},{9,10},{10,... | collective-permute-start | bytes 786440 | tf_op jit(solution)/shard_map/ppermute | solution.py:21
  63.6 7.2 %collective-permute-start.19 = (f32[1,256,256]{2,1,0:T(8,128)S(1)}, f32[1,256,256]{2,1,0:T(8,128)S(1)}, u32[]{:S(2)}, u32[]{:S(2)}) collective-permute-start(f32[1,256,256]{2,1,0:T(8,128)S(1)} %shard_map.63), channel_id=1, source_target_pairs={{0,1},{1,0},{2,3},{3,2},{4,5},{5,4},{6,7},{7,6},{8,9},{9,8},{10,11... | collective-permute-start | bytes 786440 | tf_op jit(solution)/shard_map/ppermute | solution.py:21
  71.0 7.9 %collective-permute-start.18 = (f32[256,256]{1,0:T(8,128)S(1)}, f32[256,256]{1,0:T(8,128)S(1)}, u32[]{:S(2)}, u32[]{:S(2)}) collective-permute-start(f32[256,256]{1,0:T(8,128)S(1)} %get-tuple-element.53), channel_id=1, source_target_pairs={{0,4},{1,5},{2,6},{3,7},{4,0},{5,1},{6,2},{7,3},{8,12},{9,13},{10,... | collective-permute-start | bytes 786440 | tf_op jit(solution)/shard_map/ppermute | solution.py:21
  71.6 10.9 %collective-permute-start.17 = (f32[256,256]{1,0:T(8,128)S(1)}, f32[256,256]{1,0:T(8,128)S(1)}, u32[]{:S(2)}, u32[]{:S(2)}) collective-permute-start(f32[256,256]{1,0:T(8,128)S(1)} %get-tuple-element.54), channel_id=1, source_target_pairs={{0,64},{1,65},{2,66},{3,67},{4,68},{5,69},{6,70},{7,71},{8,72},{9,... | collective-permute-start | bytes 786440 | tf_op jit(solution)/shard_map/ppermute | solution.py:21
  72.5 13.7 %collective-permute-start.20 = (f32[256,256]{1,0:T(8,128)S(1)}, f32[256,256]{1,0:T(8,128)S(1)}, u32[]{:S(2)}, u32[]{:S(2)}) collective-permute-start(f32[256,256]{1,0:T(8,128)S(1)} %get-tuple-element.56), channel_id=1, source_target_pairs={{0,68},{1,69},{2,70},{3,71},{4,64},{5,65},{6,66},{7,67},{8,76},{9,... | collective-permute-start | bytes 786440 | tf_op jit(solution)/shard_map/ppermute | solution.py:21
  74.6 11.6 %collective-permute-start.11 = (f32[256,256]{1,0:T(8,128)S(1)}, f32[256,256]{1,0:T(8,128)S(1)}, u32[]{:S(2)}, u32[]{:S(2)}) collective-permute-start(f32[256,256]{1,0:T(8,128)S(1)} %get-tuple-element.47), channel_id=1, source_target_pairs={{0,2},{1,3},{2,0},{3,1},{4,6},{5,7},{6,4},{7,5},{8,10},{9,11},{10,... | collective-permute-start | bytes 786440 | tf_op jit(solution)/shard_map/ppermute | solution.py:21
  75.5 14.3 %collective-permute-start.10 = (f32[256,256]{1,0:T(8,128)S(1)}, f32[256,256]{1,0:T(8,128)S(1)}, u32[]{:S(2)}, u32[]{:S(2)}) collective-permute-start(f32[256,256]{1,0:T(8,128)S(1)} %get-tuple-element.48), channel_id=1, source_target_pairs={{0,3},{1,2},{2,1},{3,0},{4,7},{5,6},{6,5},{7,4},{8,11},{9,10},{10,... | collective-permute-start | bytes 786440 | tf_op jit(solution)/shard_map/ppermute | solution.py:21
  78.9 11.0 %collective-permute-start.9 = (f32[256,256]{1,0:T(8,128)S(1)}, f32[256,256]{1,0:T(8,128)S(1)}, u32[]{:S(2)}, u32[]{:S(2)}) collective-permute-start(f32[256,256]{1,0:T(8,128)S(1)} %get-tuple-element.49), channel_id=1, source_target_pairs={{0,1},{1,0},{2,3},{3,2},{4,5},{5,4},{6,7},{7,6},{8,9},{9,8},{10,11... | collective-permute-start | bytes 786440 | tf_op jit(solution)/shard_map/ppermute | solution.py:21

commit v2 on v1

--- a/solution.py
+++ b/solution.py
@@ -254,7 +254,7 @@
     ]
     return total(
         [a[0], along_z(a[1], 1), along_z(a[3], 3), along_z(a[2], 2)],
-        [b[0], along_y(b[1], 1), along_y(b[2], 2), along_y(b[3], 3)],
+        [b[0], along_y(b[3], 3), along_y(b[1], 1), along_y(b[2], 2)],
     )
 
 

time: 91.1 us -> 91 us (level)
  the two profiles are of different devices: /device:TPU:5 before, /device:TPU:7 now
where the time goes in v2:
time: 91 us; the launch traced here: 90.6 us
  waiting for transfers between devices  47.9 us (53%)
  starting transfers between devices  26.7 us (29%)
  Pallas kernels  9.87 us (11%)
  blocking collectives  4.36 us (5%)
  other arithmetic  1.53 us (2%)
    ppermute x21, waiting for transfers between devices, permute(): return lax.ppermute(value, AXES, [(n, n ^ bits) for n in range(128)])  47.9 us
    ppermute x21, starting transfers between devices, permute(): return lax.ppermute(value, AXES, [(n, n ^ bits) for n in range(128)])  26.7 us
    pallas_call x2, Pallas kernels, product(): pl.pallas_call(lambda *refs: product_kernel(turns, plan, len(pieces), *re...  5.92 us
    all_to_all x1, blocking collectives, both_cores(): lax.all_to_all(jnp.broadcast_to(value[None], (2, *value.shape)), 'c', 0,...  4.36 us
    pallas_call x1, Pallas kernels, split(): pl.pallas_call(split_kernel, out_shape=[jax.ShapeDtypeStruct((8, TILE, WI...  2.76 us
  transfers between devices with their start and end apart: 21, of which 11 were waited for; matrix products, arithmetic and copies ran while one was open for 2% of the time, Pallas kernels for 10%

profile of v2, /device:TPU:7, one launch (start us, length us, event | category | flops | bytes accessed | tf_op | source)
XLA Modules:
  0.0 90.6 jit_solution(5309405903391692356)
XLA Ops:
  0.0 1.1 %collective-permute-start.2 = (f32[512,128]{1,0:T(8,128)}, f32[512,128]{1,0:T(8,128)S(1)}, u32[]{:S(2)}, u32[]{:S(2)}) collective-permute-start(f32[512,128]{1,0:T(8,128)} %param.5), channel_id=1, source_target_pairs={{0,32},{1,33},{2,34},{3,35},{4,36},{5,37},{6,38},{7,39},{8,40},{9,... | collective-permute-start | bytes 786440 | tf_op jit(solution)/shard_map/ppermute | solution.py:21
  1.1 2.1 %collective-permute-start = (f32[512,128]{1,0:T(8,128)}, f32[512,128]{1,0:T(8,128)S(1)}, u32[]{:S(2)}, u32[]{:S(2)}) collective-permute-start(f32[512,128]{1,0:T(8,128)} %param.5), channel_id=1, source_target_pairs={{0,48},{1,49},{2,50},{3,51},{4,52},{5,53},{6,54},{7,55},{8,56},{9,... | collective-permute-start | bytes 786440 | tf_op jit(solution)/shard_map/ppermute | solution.py:21
  3.3 5.7 %collective-permute-done.2 = f32[512,128]{1,0:T(8,128)S(1)} collective-permute-done((f32[512,128]{1,0:T(8,128)}, f32[512,128]{1,0:T(8,128)S(1)}, u32[]{:S(2)}, u32[]{:S(2)}) %collective-permute-start.2) | collective-permute-done | bytes 262176 | tf_op jit(solution)/shard_map/ppermute | solution.py:21
  8.9 1.0 %select_bitcast_fusion = (f32[1,512,128]{2,1,0:T(8,128)S(1)}, f32[1,512,128]{2,1,0:T(8,128)S(1)}) fusion(f32[512,128]{1,0:T(8,128)} %param.5, f32[512,128]{1,0:T(8,128)S(1)} %collective-permute-done.2, pred[]{:T(512)S(6)} %eq.3), kind=kLoop, calls=%fused_computation.25 | loop fusion | flops 131072 | bytes 1048577 | tf_op jit(solution)/shard_map/stack | solution.py:198
  9.9 2.2 %collective-permute-done.1 = f32[512,128]{1,0:T(8,128)S(1)} collective-permute-done((f32[512,128]{1,0:T(8,128)}, f32[512,128]{1,0:T(8,128)S(1)}, u32[]{:S(2)}, u32[]{:S(2)}) %collective-permute-start.1) | collective-permute-done | bytes 262176 | tf_op jit(solution)/shard_map/ppermute | solution.py:21
  12.1 3.5 %collective-permute-done = f32[512,128]{1,0:T(8,128)S(1)} collective-permute-done((f32[512,128]{1,0:T(8,128)}, f32[512,128]{1,0:T(8,128)S(1)}, u32[]{:S(2)}, u32[]{:S(2)}) %collective-permute-start) | collective-permute-done | bytes 262176 | tf_op jit(solution)/shard_map/ppermute | solution.py:21
  16.3 1.4 %collective-permute-start.3 = (f32[2,512,128]{2,1,0:T(8,128)S(1)}, f32[2,512,128]{2,1,0:T(8,128)S(1)}, u32[]{:S(2)}, u32[]{:S(2)}) collective-permute-start(f32[2,512,128]{2,1,0:T(8,128)S(1)} %pad_maximum_fusion), channel_id=1, source_target_pairs={{0,64},{1,65},{2,66},{3,67},{4,68},{5,69},{6,70},{7,71},{8,72},{9,... | collective-permute-start | bytes 1572872 | tf_op jit(solution)/shard_map/ppermute | solution.py:21
  17.7 2.8 %shard_map.55 = (bf16[8,512,256]{2,1,0:T(8,128)(2,1)S(1)}, bf16[8,512,256]{2,1,0:T(8,128)(2,1)S(1)}) custom-call(s32[5]{0:T(128)S(1)} %stack.44.spots.refs_0_, s32[2,16]{1,0:T(2,128)S(1)} %copy-done.1, s32[16,32]{1,0:T(8,128)S(1)} %copy-done, s32[2,32]{1,0:T(2,128)S(1)} %copy-done.2, f32[512,2048]{1,0:T(8,128)} %right.1), custom_call_target="tpu_custom_call" | custom-call | flops 1 | bytes 1 | tf_op jit(solution)/shard_map/pallas_call | solution.py:72
  20.5 2.5 %shard_map.56 = (f32[1,256,256]{2,1,0:T(8,128)S(1)}, f32[3,256,256]{2,1,0:T(8,128)S(1)}, f32[2,256,256]{2,1,0:T(8,128)S(1)}, f32[2,256,256]{2,1,0:T(8,128)S(1)},...) custom-call(s32[5]{0:T(128)S(1)} %stack.44.spots.refs_0_, ...), custom_call_target="tpu_custom_call" | custom-call | flops 1 | bytes 1 | tf_op jit(solution)/shard_map/pallas_call | solution.py:142
  23.0 2.5 %collective-permute-start.16 = (f32[2,256,256]{2,1,0:T(8,128)S(1)}, f32[2,256,256]{2,1,0:T(8,128)S(1)}, u32[]{:S(2)}, u32[]{:S(2)}) collective-permute-start(f32[2,256,256]{2,1,0:T(8,128)S(1)} %get-tuple-element.44), channel_id=1, source_target_pairs={{0,3},{1,2},{2,1},{3,0},{4,7},{5,6},{6,5},{7,4},{8,11},{9,10},{10,... | collective-permute-start | bytes 1572872 | tf_op jit(solution)/shard_map/ppermute | solution.py:21
  25.6 5.3 %collective-permute-start.6 = (f32[3,256,256]{2,1,0:T(8,128)S(1)}, f32[3,256,256]{2,1,0:T(8,128)S(1)}, u32[]{:S(2)}, u32[]{:S(2)}) collective-permute-start(f32[3,256,256]{2,1,0:T(8,128)S(1)} %get-tuple-element.34), channel_id=1, source_target_pairs={{0,68},{1,69},{2,70},{3,71},{4,64},{5,65},{6,66},{7,67},{8,76},{9,... | collective-permute-start | bytes 2359304 | tf_op jit(solution)/shard_map/ppermute | solution.py:21
  31.0 4.4 %all_to_all.5.refs_4_ = f32[2,2,512,128]{3,2,1,0:T(8,128)S(1)} all-to-all(f32[2,2,512,128]{3,2,1,0:T(8,128)S(1)} %broadcast_in_dim.2), channel_id=1, replica_groups=mesh['yl'=2,'x'=4,'c'=2,'yh'=2,'z'=4] {'c'}, dimensions={0} | all-to-all | bytes 2097152 | tf_op jit(solution)/shard_map/all_to_all | solution.py:187
  35.3 2.7 %collective-permute-done.5.arrived_ref = f32[1,256,256]{2,1,0:T(8,128)S(1)} collective-permute-done((f32[1,256,256]{2,1,0:T(8,128)S(1)}, f32[1,256,256]{2,1,0:T(8,128)S(1)}, u32[]{:S(2)}, u32[]{:S(2)}) %collective-permute-start.5) | collective-permute-done | bytes 262176 | tf_op jit(solution)/shard_map/ppermute | solution.py:21
  38.1 3.5 %shard_map.57 = (f32[4,256,256]{2,1,0:T(8,128)S(1)}, f32[4,256,256]{2,1,0:T(8,128)S(1)}, f32[3,256,256]{2,1,0:T(8,128)S(1)}, f32[3,256,256]{2,1,0:T(8,128)S(1)},...) custom-call(s32[5]{0:T(128)S(1)} %stack.44.spots.refs_0_, ...), custom_call_target="tpu_custom_call" | custom-call | flops 1 | bytes 1 | tf_op jit(solution)/shard_map/pallas_call | solution.py:142
  43.2 1.7 %collective-permute-start.8 = (f32[4,256,256]{2,1,0:T(8,128)S(1)}, f32[4,256,256]{2,1,0:T(8,128)S(1)}, u32[]{:S(2)}, u32[]{:S(2)}) collective-permute-start(f32[4,256,256]{2,1,0:T(8,128)S(1)} %shard_map.59), channel_id=1, source_target_pairs={{0,68},{1,69},{2,70},{3,71},{4,64},{5,65},{6,66},{7,67},{8,76},{9,... | collective-permute-start | bytes 3145736 | tf_op jit(solution)/shard_map/ppermute | solution.py:21
  45.0 2.3 %collective-permute-done.6.arrived_ref = f32[3,256,256]{2,1,0:T(8,128)S(1)} collective-permute-done((f32[3,256,256]{2,1,0:T(8,128)S(1)}, f32[3,256,256]{2,1,0:T(8,128)S(1)}, u32[]{:S(2)}, u32[]{:S(2)}) %collective-permute-start.6) | collective-permute-done | bytes 786464 | tf_op jit(solution)/shard_map/ppermute | solution.py:21
  47.5 12.5 %collective-permute-done.17.arrived_ref = f32[3,256,256]{2,1,0:T(8,128)S(1)} collective-permute-done((f32[3,256,256]{2,1,0:T(8,128)S(1)}, f32[3,256,256]{2,1,0:T(8,128)S(1)}, u32[]{:S(2)}, u32[]{:S(2)}) %collective-permute-start.17) | collective-permute-done | bytes 786464 | tf_op jit(solution)/shard_map/ppermute | solution.py:21
  60.0 2.7 %collective-permute-start.18 = (f32[1,256,256]{2,1,0:T(8,128)S(1)}, f32[1,256,256]{2,1,0:T(8,128)S(1)}, u32[]{:S(2)}, u32[]{:S(2)}) collective-permute-start(f32[1,256,256]{2,1,0:T(8,128)S(1)} %shard_map.63), channel_id=1, source_target_pairs={{0,3},{1,2},{2,1},{3,0},{4,7},{5,6},{6,5},{7,4},{8,11},{9,10},{10,... | collective-permute-start | bytes 786440 | tf_op jit(solution)/shard_map/ppermute | solution.py:21
  62.9 6.3 %collective-permute-done.18 = f32[1,256,256]{2,1,0:T(8,128)S(1)} collective-permute-done((f32[1,256,256]{2,1,0:T(8,128)S(1)}, f32[1,256,256]{2,1,0:T(8,128)S(1)}, u32[]{:S(2)}, u32[]{:S(2)}) %collective-permute-start.18) | collective-permute-done | bytes 262176 | tf_op jit(solution)/shard_map/ppermute | solution.py:21
  71.0 3.2 %collective-permute-start.20 = (f32[256,256]{1,0:T(8,128)S(1)}, f32[256,256]{1,0:T(8,128)S(1)}, u32[]{:S(2)}, u32[]{:S(2)}) collective-permute-start(f32[256,256]{1,0:T(8,128)S(1)} %get-tuple-element.56), channel_id=1, source_target_pairs={{0,4},{1,5},{2,6},{3,7},{4,0},{5,1},{6,2},{7,3},{8,12},{9,13},{10,... | collective-permute-start | bytes 786440 | tf_op jit(solution)/shard_map/ppermute | solution.py:21
  74.4 1.1 %collective-permute-start.11 = (f32[256,256]{1,0:T(8,128)S(1)}, f32[256,256]{1,0:T(8,128)S(1)}, u32[]{:S(2)}, u32[]{:S(2)}) collective-permute-start(f32[256,256]{1,0:T(8,128)S(1)} %get-tuple-element.47), channel_id=1, source_target_pairs={{0,2},{1,3},{2,0},{3,1},{4,6},{5,7},{6,4},{7,5},{8,10},{9,11},{10,... | collective-permute-start | bytes 786440 | tf_op jit(solution)/shard_map/ppermute | solution.py:21
  75.5 1.7 %collective-permute-start.10 = (f32[256,256]{1,0:T(8,128)S(1)}, f32[256,256]{1,0:T(8,128)S(1)}, u32[]{:S(2)}, u32[]{:S(2)}) collective-permute-start(f32[256,256]{1,0:T(8,128)S(1)} %get-tuple-element.48), channel_id=1, source_target_pairs={{0,3},{1,2},{2,1},{3,0},{4,7},{5,6},{6,5},{7,4},{8,11},{9,10},{10,... | collective-permute-start | bytes 786440 | tf_op jit(solution)/shard_map/ppermute | solution.py:21
  78.5 5.9 %collective-permute-done.20.refs_7_ = f32[256,256]{1,0:T(8,128)S(1)} collective-permute-done((f32[256,256]{1,0:T(8,128)S(1)}, f32[256,256]{1,0:T(8,128)S(1)}, u32[]{:S(2)}, u32[]{:S(2)}) %collective-permute-start.20) | collective-permute-done | bytes 262176 | tf_op jit(solution)/shard_map/ppermute | solution.py:21
  84.3 5.3 %collective-permute-done.10.refs_2_ = f32[256,256]{1,0:T(8,128)S(1)} collective-permute-done((f32[256,256]{1,0:T(8,128)S(1)}, f32[256,256]{1,0:T(8,128)S(1)}, u32[]{:S(2)}, u32[]{:S(2)}) %collective-permute-start.10) | collective-permute-done | bytes 262176 | tf_op jit(solution)/shard_map/ppermute | solution.py:21
  (43 shorter events, 7.2 us)
Async XLA Ops:
  0.0 8.9 %collective-permute-start.2 = (f32[512,128]{1,0:T(8,128)}, f32[512,128]{1,0:T(8,128)S(1)}, u32[]{:S(2)}, u32[]{:S(2)}) collective-permute-start(f32[512,128]{1,0:T(8,128)} %param.5), channel_id=1, source_target_pairs={{0,32},{1,33},{2,34},{3,35},{4,36},{5,37},{6,38},{7,39},{8,40},{9,... | collective-permute-start | bytes 786440 | tf_op jit(solution)/shard_map/ppermute | solution.py:21
  1.1 11.0 %collective-permute-start.1 = (f32[512,128]{1,0:T(8,128)}, f32[512,128]{1,0:T(8,128)S(1)}, u32[]{:S(2)}, u32[]{:S(2)}) collective-permute-start(f32[512,128]{1,0:T(8,128)} %param.5), channel_id=1, source_target_pairs={{0,16},{1,17},{2,18},{3,19},{4,20},{5,21},{6,22},{7,23},{8,24},{9,... | collective-permute-start | bytes 786440 | tf_op jit(solution)/shard_map/ppermute | solution.py:21
  1.1 14.4 %collective-permute-start = (f32[512,128]{1,0:T(8,128)}, f32[512,128]{1,0:T(8,128)S(1)}, u32[]{:S(2)}, u32[]{:S(2)}) collective-permute-start(f32[512,128]{1,0:T(8,128)} %param.5), channel_id=1, source_target_pairs={{0,48},{1,49},{2,50},{3,51},{4,52},{5,53},{6,54},{7,55},{8,56},{9,... | collective-permute-start | bytes 786440 | tf_op jit(solution)/shard_map/ppermute | solution.py:21
  3.3 14.5 %copy-start = (s32[16,32]{1,0:T(8,128)S(1)}, s32[16,32]{1,0:T(8,128)}, u32[]{:S(2)}) copy-start(s32[16,32]{1,0:T(8,128)} %refs_2_.3) | copy-start | bytes 6148
  3.3 14.5 %copy-start.1 = (s32[2,16]{1,0:T(2,128)S(1)}, s32[2,16]{1,0:T(2,128)}, u32[]{:S(2)}) copy-start(s32[2,16]{1,0:T(2,128)} %refs_1_.3) | copy-start | bytes 388
  3.3 14.5 %copy-start.2 = (s32[2,32]{1,0:T(2,128)S(1)}, s32[2,32]{1,0:T(2,128)}, u32[]{:S(2)}) copy-start(s32[2,32]{1,0:T(2,128)} %refs_3_.3) | copy-start | bytes 772
  15.6 4.8 %collective-permute-start.4 = (f32[2,512,128]{2,1,0:T(8,128)S(1)}, f32[2,512,128]{2,1,0:T(8,128)S(1)}, u32[]{:S(2)}, u32[]{:S(2)}) collective-permute-start(f32[2,512,128]{2,1,0:T(8,128)S(1)} %pad_maximum_fusion.1.refs_4_), channel_id=1, source_target_pairs={{0,8},{1,9},{2,10},{3,11},{4,12},{5,13},{6,14},{7,15},{8,0},{9,1},... | collective-permute-start | bytes 1572872 | tf_op jit(solution)/shard_map/ppermute | solution.py:21
  16.3 14.6 %collective-permute-start.3 = (f32[2,512,128]{2,1,0:T(8,128)S(1)}, f32[2,512,128]{2,1,0:T(8,128)S(1)}, u32[]{:S(2)}, u32[]{:S(2)}) collective-permute-start(f32[2,512,128]{2,1,0:T(8,128)S(1)} %pad_maximum_fusion), channel_id=1, source_target_pairs={{0,64},{1,65},{2,66},{3,67},{4,68},{5,69},{6,70},{7,71},{8,72},{9,... | collective-permute-start | bytes 1572872 | tf_op jit(solution)/shard_map/ppermute | solution.py:21
  23.0 18.6 %collective-permute-start.16 = (f32[2,256,256]{2,1,0:T(8,128)S(1)}, f32[2,256,256]{2,1,0:T(8,128)S(1)}, u32[]{:S(2)}, u32[]{:S(2)}) collective-permute-start(f32[2,256,256]{2,1,0:T(8,128)S(1)} %get-tuple-element.44), channel_id=1, source_target_pairs={{0,3},{1,2},{2,1},{3,0},{4,7},{5,6},{6,5},{7,4},{8,11},{9,10},{10,... | collective-permute-start | bytes 1572872 | tf_op jit(solution)/shard_map/ppermute | solution.py:21
  25.4 16.9 %collective-permute-start.12 = (f32[2,256,256]{2,1,0:T(8,128)S(1)}, f32[2,256,256]{2,1,0:T(8,128)S(1)}, u32[]{:S(2)}, u32[]{:S(2)}) collective-permute-start(f32[2,256,256]{2,1,0:T(8,128)S(1)} %get-tuple-element.38), channel_id=1, source_target_pairs={{0,1},{1,0},{2,3},{3,2},{4,5},{5,4},{6,7},{7,6},{8,9},{9,8},{10,11... | collective-permute-start | bytes 1572872 | tf_op jit(solution)/shard_map/ppermute | solution.py:21
  25.6 21.7 %collective-permute-start.6 = (f32[3,256,256]{2,1,0:T(8,128)S(1)}, f32[3,256,256]{2,1,0:T(8,128)S(1)}, u32[]{:S(2)}, u32[]{:S(2)}) collective-permute-start(f32[3,256,256]{2,1,0:T(8,128)S(1)} %get-tuple-element.34), channel_id=1, source_target_pairs={{0,68},{1,69},{2,70},{3,71},{4,64},{5,65},{6,66},{7,67},{8,76},{9,... | collective-permute-start | bytes 2359304 | tf_op jit(solution)/shard_map/ppermute | solution.py:21
  30.9 7.2 %collective-permute-start.5 = (f32[1,256,256]{2,1,0:T(8,128)S(1)}, f32[1,256,256]{2,1,0:T(8,128)S(1)}, u32[]{:S(2)}, u32[]{:S(2)}) collective-permute-start(f32[1,256,256]{2,1,0:T(8,128)S(1)} %get-tuple-element.31), channel_id=1, source_target_pairs={{0,64},{1,65},{2,66},{3,67},{4,68},{5,69},{6,70},{7,71},{8,72},{9,... | collective-permute-start | bytes 786440 | tf_op jit(solution)/shard_map/ppermute | solution.py:21
  41.6 18.4 %collective-permute-start.17 = (f32[3,256,256]{2,1,0:T(8,128)S(1)}, f32[3,256,256]{2,1,0:T(8,128)S(1)}, u32[]{:S(2)}, u32[]{:S(2)}) collective-permute-start(f32[3,256,256]{2,1,0:T(8,128)S(1)} %shard_map.62), channel_id=1, source_target_pairs={{0,1},{1,0},{2,3},{3,2},{4,5},{5,4},{6,7},{7,6},{8,9},{9,8},{10,11... | collective-permute-start | bytes 2359304 | tf_op jit(solution)/shard_map/ppermute | solution.py:21
  42.4 20.4 %collective-permute-start.13 = (f32[3,256,256]{2,1,0:T(8,128)S(1)}, f32[3,256,256]{2,1,0:T(8,128)S(1)}, u32[]{:S(2)}, u32[]{:S(2)}) collective-permute-start(f32[3,256,256]{2,1,0:T(8,128)S(1)} %shard_map.60), channel_id=1, source_target_pairs={{0,3},{1,2},{2,1},{3,0},{4,7},{5,6},{6,5},{7,4},{8,11},{9,10},{10,... | collective-permute-start | bytes 2359304 | tf_op jit(solution)/shard_map/ppermute | solution.py:21
  43.2 31.0 %collective-permute-start.8 = (f32[4,256,256]{2,1,0:T(8,128)S(1)}, f32[4,256,256]{2,1,0:T(8,128)S(1)}, u32[]{:S(2)}, u32[]{:S(2)}) collective-permute-start(f32[4,256,256]{2,1,0:T(8,128)S(1)} %shard_map.59), channel_id=1, source_target_pairs={{0,68},{1,69},{2,70},{3,71},{4,64},{5,65},{6,66},{7,67},{8,76},{9,... | collective-permute-start | bytes 3145736 | tf_op jit(solution)/shard_map/ppermute | solution.py:21
  47.4 26.8 %collective-permute-start.7 = (f32[4,256,256]{2,1,0:T(8,128)S(1)}, f32[4,256,256]{2,1,0:T(8,128)S(1)}, u32[]{:S(2)}, u32[]{:S(2)}) collective-permute-start(f32[4,256,256]{2,1,0:T(8,128)S(1)} %shard_map.58), channel_id=1, source_target_pairs={{0,64},{1,65},{2,66},{3,67},{4,68},{5,69},{6,70},{7,71},{8,72},{9,... | collective-permute-start | bytes 3145736 | tf_op jit(solution)/shard_map/ppermute | solution.py:21
  60.0 9.1 %collective-permute-start.18 = (f32[1,256,256]{2,1,0:T(8,128)S(1)}, f32[1,256,256]{2,1,0:T(8,128)S(1)}, u32[]{:S(2)}, u32[]{:S(2)}) collective-permute-start(f32[1,256,256]{2,1,0:T(8,128)S(1)} %shard_map.63), channel_id=1, source_target_pairs={{0,3},{1,2},{2,1},{3,0},{4,7},{5,6},{6,5},{7,4},{8,11},{9,10},{10,... | collective-permute-start | bytes 786440 | tf_op jit(solution)/shard_map/ppermute | solution.py:21
  62.8 7.3 %collective-permute-start.14 = (f32[1,256,256]{2,1,0:T(8,128)S(1)}, f32[1,256,256]{2,1,0:T(8,128)S(1)}, u32[]{:S(2)}, u32[]{:S(2)}) collective-permute-start(f32[1,256,256]{2,1,0:T(8,128)S(1)} %shard_map.61), channel_id=1, source_target_pairs={{0,1},{1,0},{2,3},{3,2},{4,5},{5,4},{6,7},{7,6},{8,9},{9,8},{10,11... | collective-permute-start | bytes 786440 | tf_op jit(solution)/shard_map/ppermute | solution.py:21
  70.3 7.6 %collective-permute-start.15 = (f32[256,256]{1,0:T(8,128)S(1)}, f32[256,256]{1,0:T(8,128)S(1)}, u32[]{:S(2)}, u32[]{:S(2)}) collective-permute-start(f32[256,256]{1,0:T(8,128)S(1)} %get-tuple-element.53), channel_id=1, source_target_pairs={{0,68},{1,69},{2,70},{3,71},{4,64},{5,65},{6,66},{7,67},{8,76},{9,... | collective-permute-start | bytes 786440 | tf_op jit(solution)/shard_map/ppermute | solution.py:21
  70.4 8.1 %collective-permute-start.19 = (f32[256,256]{1,0:T(8,128)S(1)}, f32[256,256]{1,0:T(8,128)S(1)}, u32[]{:S(2)}, u32[]{:S(2)}) collective-permute-start(f32[256,256]{1,0:T(8,128)S(1)} %get-tuple-element.55), channel_id=1, source_target_pairs={{0,64},{1,65},{2,66},{3,67},{4,68},{5,69},{6,70},{7,71},{8,72},{9,... | collective-permute-start | bytes 786440 | tf_op jit(solution)/shard_map/ppermute | solution.py:21
  71.0 13.4 %collective-permute-start.20 = (f32[256,256]{1,0:T(8,128)S(1)}, f32[256,256]{1,0:T(8,128)S(1)}, u32[]{:S(2)}, u32[]{:S(2)}) collective-permute-start(f32[256,256]{1,0:T(8,128)S(1)} %get-tuple-element.56), channel_id=1, source_target_pairs={{0,4},{1,5},{2,6},{3,7},{4,0},{5,1},{6,2},{7,3},{8,12},{9,13},{10,... | collective-permute-start | bytes 786440 | tf_op jit(solution)/shard_map/ppermute | solution.py:21
  74.4 9.9 %collective-permute-start.11 = (f32[256,256]{1,0:T(8,128)S(1)}, f32[256,256]{1,0:T(8,128)S(1)}, u32[]{:S(2)}, u32[]{:S(2)}) collective-permute-start(f32[256,256]{1,0:T(8,128)S(1)} %get-tuple-element.47), channel_id=1, source_target_pairs={{0,2},{1,3},{2,0},{3,1},{4,6},{5,7},{6,4},{7,5},{8,10},{9,11},{10,... | collective-permute-start | bytes 786440 | tf_op jit(solution)/shard_map/ppermute | solution.py:21
  75.5 14.2 %collective-permute-start.10 = (f32[256,256]{1,0:T(8,128)S(1)}, f32[256,256]{1,0:T(8,128)S(1)}, u32[]{:S(2)}, u32[]{:S(2)}) collective-permute-start(f32[256,256]{1,0:T(8,128)S(1)} %get-tuple-element.48), channel_id=1, source_target_pairs={{0,3},{1,2},{2,1},{3,0},{4,7},{5,6},{6,5},{7,4},{8,11},{9,10},{10,... | collective-permute-start | bytes 786440 | tf_op jit(solution)/shard_map/ppermute | solution.py:21
  77.8 11.9 %collective-permute-start.9 = (f32[256,256]{1,0:T(8,128)S(1)}, f32[256,256]{1,0:T(8,128)S(1)}, u32[]{:S(2)}, u32[]{:S(2)}) collective-permute-start(f32[256,256]{1,0:T(8,128)S(1)} %get-tuple-element.49), channel_id=1, source_target_pairs={{0,1},{1,0},{2,3},{3,2},{4,5},{5,4},{6,7},{7,6},{8,9},{9,8},{10,11... | collective-permute-start | bytes 786440 | tf_op jit(solution)/shard_map/ppermute | solution.py:21
